TPU v7x, 128 devices: a whole 4x4x4 slice. The times are simulated.
128 devices in a mesh: row: 8 (over y, x_lo), col: 16 (over z, x_hi, core).
Axes of the slice: x: 4 (x_hi: 2, x_lo: 2; x = x_hi * 2 + x_lo), y: 4, z: 4, core: 2. Of those that a mesh axis runs over, the one named last changes fastest.
Arguments:
- tokens: bfloat16 [16384, 3584], P(('row', 'col')), may hold values from -6 to 6
- expert_ids: int32 [16384, 4], P(('row', 'col')), may hold values from 0 to 127, all different within a row; in each aligned block of 128 rows (0 to 127, 128 to 255, ...) at most 5 rows name the same one
- combine_weights: float32 [16384, 4], P(('row', 'col')), may hold values from 0.1 to 1
- expert_gate: bfloat16 [128, 3584, 1024], P(('row', 'col')), may hold values from -0.09375 to 0.09375
- expert_up: bfloat16 [128, 3584, 1024], P(('row', 'col')), may hold values from -0.09375 to 0.09375
- expert_down: bfloat16 [128, 1024, 3584], P(('row', 'col')), may hold values from -0.1875 to 0.1875
- shared_gate: bfloat16 [3584, 1024], P(None, 'row'), may hold values from -0.09375 to 0.09375
- shared_up: bfloat16 [3584, 1024], P(None, 'row'), may hold values from -0.09375 to 0.09375
- shared_down: bfloat16 [1024, 3584], P('row'), may hold values from -0.1875 to 0.1875
Outputs:
- mixed: bfloat16 [16384, 3584], P(('row', 'col'))
Inputs may be any that keep to these rules, and one draw needn't show every extreme that they name: `expert_ids`: each row names 4 different experts. Among the 128 rows of one device no expert is named by more than 5 rows, and in every draw some expert is named by exactly 5 rows of some device.
All inputs are finite; a program needn't handle non-finite values.
Results may differ from a plain program's by a relative error of at most 0.0055.
Values may be sent and summed in bfloat16 or wider, within the bound.
A program may use at most 128 MiB of HBM per device.

v0:
```python
import jax
import jax.numpy as jnp
from jax import lax
from jax.sharding import Mesh
from jax.sharding import PartitionSpec as P

ROW = ("row_0", "row_1")
ROW_COL = ("row_0", "row_1", "col")


def own_rows(running, axes):
    for axis in axes:
        running = lax.psum_scatter(running, axis, scatter_dimension=0, tiled=True)
    return running


def expert_mlp(token_rows, gate_w, up_w, down_w):
    gate_proj = jnp.dot(token_rows, gate_w, preferred_element_type=jnp.float32)
    up_proj = jnp.dot(token_rows, up_w, preferred_element_type=jnp.float32)
    hidden = (jax.nn.silu(gate_proj) * up_proj).astype(jnp.bfloat16)
    return jnp.dot(hidden, down_w, preferred_element_type=jnp.float32).astype(jnp.bfloat16)


def place_slots(choices, experts, capacity):
    flat_ids = choices.reshape(-1)
    onehot = (flat_ids[:, None] == jnp.arange(experts, dtype=jnp.int32)[None, :]).astype(jnp.int32)
    running = jnp.cumsum(onehot, axis=0)
    slot_rank = jnp.sum(onehot * running, axis=1) - 1
    return flat_ids * capacity + slot_rank


def per_device(
    tokens,
    expert_ids,
    combine_weights,
    expert_gate,
    expert_up,
    expert_down,
    shared_gate,
    shared_up,
    shared_down,
):
    rows_here, model_width = tokens.shape
    choices_each = expert_ids.shape[1]
    row_devices = lax.axis_size(ROW)
    col_devices = lax.axis_size("col")
    experts = row_devices * col_devices
    capacity = max(2, 5 * rows_here * choices_each // (4 * experts))
    target = place_slots(expert_ids, experts, capacity)
    owner_row = jnp.arange(rows_here * choices_each, dtype=jnp.int32) // choices_each
    source_table = jnp.full((experts * capacity,), -1, jnp.int32).at[target].set(owner_row)
    filled = source_table >= 0
    outgoing = jnp.where(
        filled[:, None], tokens[jnp.maximum(source_table, 0)], jnp.zeros((), jnp.bfloat16)
    )
    arrived = lax.all_to_all(
        outgoing.reshape(experts, capacity, model_width),
        ROW_COL,
        split_axis=0,
        concat_axis=0,
        tiled=True,
    )
    results = expert_mlp(
        arrived.reshape(-1, model_width), expert_gate[0], expert_up[0], expert_down[0]
    )
    returned = lax.all_to_all(
        results.reshape(experts, capacity, model_width),
        ROW_COL,
        split_axis=0,
        concat_axis=0,
        tiled=True,
    )
    returned = returned.reshape(-1, model_width)
    picked = returned[target].reshape(rows_here, choices_each, model_width)
    routed = jnp.sum(picked.astype(jnp.float32) * combine_weights[:, :, None], axis=1)
    shard_rows = lax.all_gather(tokens, ROW, axis=0, tiled=True)
    gate_proj = jnp.dot(shard_rows, shared_gate, preferred_element_type=jnp.float32)
    up_proj = jnp.dot(shard_rows, shared_up, preferred_element_type=jnp.float32)
    shared_hidden = (jax.nn.silu(gate_proj) * up_proj).astype(jnp.bfloat16)
    shared = own_rows(jnp.dot(shared_hidden, shared_down, preferred_element_type=jnp.float32), ROW)
    return (routed + shared).astype(jnp.bfloat16)


def solution(mesh):
    finer = Mesh(mesh.devices.reshape(4, 2, mesh.shape["col"]), ("row_0", "row_1", "col"))
    placed = (
        P(ROW_COL, None),
        P(ROW_COL, None),
        P(ROW_COL, None),
        P(ROW_COL, None, None),
        P(ROW_COL, None, None),
        P(ROW_COL, None, None),
        P(None, ROW),
        P(None, ROW),
        P(ROW, None),
    )
    return jax.shard_map(
        per_device, mesh=finer, in_specs=placed, out_specs=P(ROW_COL, None), check_vma=False
    )
```

profile of v0, /device:TPU:1, one launch (start us, length us, event | category | flops | bytes accessed | tf_op | source)
XLA Modules:
  0.0 583.5 jit_solution(16821377509099226746)
XLA Ops:
  6.5 0.7 all-gather.2.cloned.1.call-update
  7.3 153.6 %all-gather.2.cloned.1.call-done = bf16[1024,3584]{1,0:T(8,128)(2,1)} async-done(((bf16[128,3584]{1,0:T(8,128)(2,1)}), bf16[1024,3584]{1,0:T(8,128)(2,1)}) %all-gather.2.cloned.1.call-update) | async-done | bytes 7340048 | tf_op jit(solution)/shard_map/all_gather | solution.py:76
  160.9 5.3 fusion.33
  166.2 15.9 %fusion.15 = f32[1024,3584]{1,0:T(8,128)} fusion(bf16[128,3584]{1,0:T(8,128)(2,1)S(1)} %copy-done, bf16[1024,3584]{1,0:T(8,128)(2,1)} %all-gather.2.cloned.1.call-done, bf16[3584,128]{1,0:T(8,128)(2,1)S(1)} %copy-done.3, f32[1024,128]{1,0:T(8,128)S(1)} %fusion.33), kind=kOutput, calls=%fused_computation.17 | convolution fusion | flops 1879834624 | bytes 24379392 | tf_op jit(solution)/shard_map/dot_general | solution.py:80
  182.2 0.6 copy-done.4
  182.8 0.1 copy.12
  182.9 0.1 eq.29
  183.0 0.1 eq.25
  183.2 0.1 copy.11
  183.3 0.1 mul.43
  183.4 0.1 copy.14
  183.5 0.2 fusion.23
  183.8 0.2 fusion.21
  184.1 2.4 scatter_custom_fusion
  186.5 0.2 broadcast_in_dim.26
  186.8 5.2 gather_fusion
  192.0 8.1 %gather.9 = bf16[128,5,3584]{2,1,0:T(8,128)(2,1)} reshape(bf16[640,3584]{1,0:T(8,128)(2,1)} %gather_fusion) | data formatting | bytes 9175040 | tf_op jit(solution)/shard_map/gather | solution.py:54
  200.1 4.0 broadcast_select_fusion
  204.1 112.0 %all_to_all.10 = bf16[128,5,3584]{2,1,0:T(8,128)(2,1)} all-to-all(bf16[128,5,3584]{2,1,0:T(8,128)(2,1)S(1)} %broadcast_select_fusion), channel_id=1, replica_groups=mesh['row_0'=4,'row_1'=2,'col'=16] {'row_0','row_1','col'}, dimensions={0} | all-to-all | bytes 9175040 | tf_op jit(solution)/shard_map/all_to_all | solution.py:56
  316.1 8.3 %reshape.73 = bf16[640,3584]{1,0:T(8,128)(2,1)} reshape(bf16[128,5,3584]{2,1,0:T(8,128)(2,1)} %all_to_all.10) | data formatting | bytes 9175040 | tf_op jit(solution)/shard_map/reshape | solution.py:64
  324.3 69.2 %reduce-scatter.3.cloned.1.call-done = f32[256,3584]{1,0:T(8,128)} async-done(((f32[1024,3584]{1,0:T(8,128)}), f32[256,3584]{1,0:T(8,128)}) %reduce-scatter.3.cloned.1.call-update) | async-done | bytes 3670032 | tf_op jit(solution)/shard_map/reduce_scatter | solution.py:13
  393.6 10.9 %fusion.4 = f32[640,1024]{1,0:T(8,128)} fusion(bf16[640,3584]{1,0:T(8,128)(2,1)} %reshape.73, bf16[1,3584,1024]{2,1,0:T(8,128)(2,1)} %param.12), kind=kOutput, calls=%fused_computation.7 | convolution fusion | flops 4697620480 | bytes 14548992 | tf_op jit(solution)/shard_map/dot_general | solution.py:18
  404.5 18.8 %fusion.6 = bf16[640,3584]{1,0:T(8,128)(2,1)} fusion(bf16[1,1024,3584]{2,1,0:T(8,128)(2,1)} %param.14, f32[640,1024]{1,0:T(8,128)} %fusion.4, bf16[640,3584]{1,0:T(8,128)(2,1)} %reshape.73, bf16[1,3584,1024]{2,1,0:T(8,128)(2,1)} %param.13), kind=kOutput, calls=%fused_computation.11 | convolution fusion | flops 9401466880 | bytes 26476544 | tf_op jit(solution)/shard_map/dot_general | solution.py:21
  423.3 7.8 %reshape.74 = bf16[128,5,3584]{2,1,0:T(8,128)(2,1)} reshape(bf16[640,3584]{1,0:T(8,128)(2,1)} %fusion.6) | data formatting | bytes 9175040 | tf_op jit(solution)/shard_map/reshape | solution.py:67
  431.1 11.8 %all-to-all-start.1 = ((bf16[128,5,3584]{2,1,0:T(8,128)(2,1)}), bf16[128,5,3584]{2,1,0:T(8,128)(2,1)}, u32[]{:S(2)}, u32[]{:S(2)}) async-start(bf16[128,5,3584]{2,1,0:T(8,128)(2,1)} %reshape.74), calls=%async_computation.1 | async-start | bytes 14680064 | tf_op jit(solution)/shard_map/all_to_all | solution.py:66
  442.9 0.1 copy.16
  443.1 96.6 %all-to-all-done.1 = bf16[128,5,3584]{2,1,0:T(8,128)(2,1)} async-done(((bf16[128,5,3584]{2,1,0:T(8,128)(2,1)}), bf16[128,5,3584]{2,1,0:T(8,128)(2,1)}, u32[]{:S(2)}, u32[]{:S(2)}) %all-to-all-start.1) | async-done | bytes 4587552 | tf_op jit(solution)/shard_map/all_to_all | solution.py:66
  539.6 8.1 %reshape.75 = bf16[640,3584]{1,0:T(8,128)(2,1)} reshape(bf16[128,5,3584]{2,1,0:T(8,128)(2,1)} %all-to-all-done.1) | data formatting | bytes 9175040 | tf_op jit(solution)/shard_map/reshape | solution.py:73
  547.8 10.8 %gather_fusion.1 = bf16[512,3584]{1,0:T(8,128)(2,1)} fusion(bf16[640,3584]{1,0:T(8,128)(2,1)} %reshape.75, s32[1024]{0:T(1024)S(1)} %pad_clamp_fusion), kind=kCustom, calls=%fused_computation.1 | custom fusion | bytes 7342080 | tf_op jit(solution)/shard_map/gather | solution.py:74
  558.5 7.5 %reshape.76 = f32[128,4,3584]{2,1,0:T(4,128)} reshape(bf16[512,3584]{1,0:T(8,128)(2,1)} %gather_fusion.1) | data formatting | bytes 11010048 | tf_op jit(solution)/shard_map/convert_element_type | solution.py:75
  566.0 8.3 %multiply_reduce_fusion = f32[128,3584]{1,0:T(8,128)S(1)} fusion(f32[128,4,3584]{2,1,0:T(4,128)} %reshape.76, f32[128,4]{1,0:T(8,128)S(1)} %copy.16), kind=kLoop, calls=%fused_computation.9 | loop fusion | flops 3211264 | bytes 9177088 | tf_op jit(solution)/shard_map/reduce_sum | solution.py:75
  574.4 2.6 add_convert_fusion
  (31 shorter events, 0.3 us)
Async XLA Ops:
  6.5 159.7 %copy-start = (bf16[128,3584]{1,0:T(8,128)(2,1)S(1)}, bf16[128,3584]{1,0:T(8,128)(2,1)}, u32[]{:S(2)}) copy-start(bf16[128,3584]{1,0:T(8,128)(2,1)} %param.17) | copy-start | bytes 2752516
  6.5 154.4 %all-gather.2.cloned.1.call-start = ((), (), s32[]{:S(2)}) async-start(), calls=%async_computation.4 | async-start | bytes 8257536 | tf_op jit(solution)/shard_map/all_gather | solution.py:76
  7.3 159.0 %copy-start.3 = (bf16[3584,128]{1,0:T(8,128)(2,1)S(1)}, bf16[3584,128]{1,0:T(8,128)(2,1)}, u32[]{:S(2)}) copy-start(bf16[3584,128]{1,0:T(8,128)(2,1)} %param.16) | copy-start | bytes 2752516
  7.3 386.3 %reduce-scatter.3.cloned.1.call-start = ((), (), s32[]{:S(2)}) async-start(), calls=%async_computation.5 | async-start | bytes 18350080 | tf_op jit(solution)/shard_map/reduce_scatter | solution.py:13
  182.1 0.7 copy-start.4
  182.2 4.6 copy-start.2
  182.2 392.2 %reduce-scatter.5.cloned.1.call-start = ((), (), s32[]{:S(2)}) async-start(), calls=%async_computation.6 | async-start | bytes 5505024 | tf_op jit(solution)/shard_map/reduce_scatter | solution.py:13
  431.1 11.8 %copy-start.5 = (f32[128,4]{0,1:T(4,128)S(1)}, f32[128,4]{0,1:T(4,128)}, u32[]{:S(2)}) copy-start(f32[128,4]{0,1:T(4,128)} %param.11) | copy-start | bytes 6148
  431.1 108.5 %all-to-all-start.1 = ((bf16[128,5,3584]{2,1,0:T(8,128)(2,1)}), bf16[128,5,3584]{2,1,0:T(8,128)(2,1)}, u32[]{:S(2)}, u32[]{:S(2)}) async-start(bf16[128,5,3584]{2,1,0:T(8,128)(2,1)} %reshape.74), calls=%async_computation.1 | async-start | bytes 14680064 | tf_op jit(solution)/shard_map/all_to_all | solution.py:66
  566.0 10.9 %copy-start.1 = (bf16[128,3584]{1,0:T(8,128)(2,1)S(1)}, bf16[128,3584]{1,0:T(8,128)(2,1)}, u32[]{:S(2)}) copy-start(bf16[128,3584]{1,0:T(8,128)(2,1)} %param.17) | copy-start | bytes 2752516
Sparse Core Ops, SparseCore 0:
  9.0 151.8 all-gather.1
  182.3 211.2 reduce-scatter.2
  395.9 58.9 reduce-scatter.4
where the time goes:
time: 590 us; the launch traced here: 584 us
  waiting for transfers between devices  320 us (54%)
  blocking collectives  112 us (19%)
  local copies, waits for them, and re-layouts  59.9 us (10%)
  matrix products  50.9 us (9%)
  other arithmetic  15.4 us (3%)
  between operations  13.3 us (2%)
  starting transfers between devices  11.9 us (2%)
    all_gather x1, waiting for transfers between devices, per_device(): shard_rows = lax.all_gather(tokens, ROW, axis=0, tiled=True)  154 us
    all_to_all x1, blocking collectives, per_device(): lax.all_to_all(outgoing.reshape(experts, capacity, model_width), ROW_COL,...  112 us
    all_to_all x1, waiting for transfers between devices, per_device(): lax.all_to_all(results.reshape(experts, capacity, model_width), ROW_COL,...  96.6 us
    reduce_scatter x2, waiting for transfers between devices, own_rows(): running = lax.psum_scatter(running, axis, scatter_dimension=0, tiled=True)  69.2 us
    dot_general x1, matrix products, expert_mlp(): jnp.dot(hidden, down_w, preferred_element_type=jnp.float32)  18.8 us
    dot_general x1, matrix products, per_device(): jnp.dot(shared_hidden, shared_down, preferred_element_type=jnp.float32)  15.9 us
    gather x2, local copies, waits for them, and re-layouts, per_device(): tokens[jnp.maximum(source_table, 0)]  13.3 us
    all_to_all x1, starting transfers between devices, per_device(): lax.all_to_all(results.reshape(experts, capacity, model_width), ROW_COL,...  11.8 us
  transfers between devices with their start and end apart: 4, of which 3 were waited for; matrix products, arithmetic and copies ran while one was open for 17% of the time, Pallas kernels for 0%

commit v1 on v0

v1 whole, which is shorter than its diff:
```python
import functools

import jax
import jax.numpy as jnp
from jax import lax
from jax.experimental import pallas as pl
from jax.experimental.pallas import tpu as pltpu
from jax.sharding import PartitionSpec as P

D = 3584
FF = 1024
T = 128
CAP = 5
DC = 512
NC = D // DC
PEERS = 16
SRC = 8
ROWS = CAP * SRC
ALL = PEERS * ROWS
LAG_B = 2
LAG_R = 2
LAG_F = 1
MESH = pl.DeviceIdType.MESH
bf16 = jnp.bfloat16
f32 = jnp.float32


def kernel(
    tok_hbm, meta_hbm, wg_hbm, wu_hbm, wd_hbm, sg_hbm, su_hbm, sd_hbm,
    out_ref,
    tok, snd, arr, ret, stage, acc, hid, pmat, cmat, wgu, wdn, wsh, wsd, sacc, shid,
    psend, prcv, ysend, yrcv, oacc, mt,
    ld, g_s, g_r, b_s, b_r, m_l, m_s, m_r, mb, a_s, a_r, r_s, r_r, w_s, w_l, wg_l, wd_l, p_s, p_r, y_s, y_r,
):
    row = lax.axis_index("row")
    col = lax.axis_index("col")
    y, x_lo = row // 2, row % 2
    z, x_hi, k = col // 4, (col // 2) % 2, col % 2
    x = x_hi * 2 + x_lo

    def dev(dx, dy, dz, dk):
        xx, yy, zz, kk = (x + dx) % 4, (y + dy) % 4, (z + dz) % 4, (k + dk) % 2
        return (yy * 2 + xx % 2, zz * 4 + (xx // 2) * 2 + kk)

    def remote(src, dst, ssem, rsem, where):
        return pltpu.make_async_remote_copy(
            src, dst, ssem, rsem, device_id=where, device_id_type=MESH
        )

    def wait_bytes(ref, sem):
        pltpu.make_async_copy(ref, ref, sem).wait()

    native = x_lo == k

    def tok_load(c):
        return pltpu.make_async_copy(
            tok_hbm.at[:, pl.ds(c * DC, DC)], tok.at[c, 0], ld.at[c]
        )

    meta_copy = pltpu.make_async_copy(meta_hbm, mt.at[0], m_l)
    meta_copy.start()
    for c in range(NC):
        tok_load(c).start()

    def wgu_load(c, slot):
        rows = pl.ds(c * DC, DC)
        return (
            pltpu.make_async_copy(wg_hbm.at[rows, :], wgu.at[slot, :, pl.ds(0, FF)], wg_l.at[slot, 0]),
            pltpu.make_async_copy(wu_hbm.at[rows, :], wgu.at[slot, :, pl.ds(FF, FF)], wg_l.at[slot, 1]),
        )

    def wdn_load(n, slot):
        return pltpu.make_async_copy(
            wd_hbm.at[:, pl.ds(n * DC, DC)], wdn.at[slot], wd_l.at[slot]
        )

    for slot in range(2):
        for copy in wgu_load(slot, slot):
            copy.start()
        wdn_load(slot, slot).start()

    barrier = pltpu.get_barrier_semaphore()
    plane = [(i // 4, 0, i % 4, 0) for i in range(1, PEERS)]
    friends = plane + [(0, 1, 0, 0), (0, 2, 0, 0), (0, 3, 0, 0), (0, 0, 0, 1)]
    for offset in friends:
        pl.semaphore_signal(barrier, inc=1, device_id=dev(*offset), device_id_type=MESH)
    pl.semaphore_wait(barrier, len(friends))

    meta_copy.wait()

    def meta_send(dy):
        return remote(mt.at[0], mt.at[4 - dy], m_s.at[dy], m_r.at[4 - dy], dev(0, dy, 0, 0))

    for dy in range(1, 4):
        meta_send(dy).start()

    def gather_send(c, dy):
        return remote(
            tok.at[c, 0], tok.at[c, 4 - dy], g_s.at[c, dy], g_r.at[c, 4 - dy], dev(0, dy, 0, 0)
        )

    def gather_start(c):
        tok_load(c).wait()
        for dy in range(1, 4):
            gather_send(c, dy).start()

    for c in range(2):
        gather_start(c)

    def shared_pieces():
        lanes = (pl.ds(0, 128), pl.ds(128, 128))
        return (
            (sg_hbm, wsh.at[:, :, lanes[0]], 1),
            (su_hbm, wsh.at[:, :, lanes[1]], 3),
            (sd_hbm.at[pl.ds(0, 64)], wsd.at[pl.ds(0, 64)], 1),
            (sd_hbm.at[pl.ds(64, 64)], wsd.at[pl.ds(64, 64)], 3),
        )

    @pl.when(native)
    def _():
        for i, (src, dst, dx) in enumerate(shared_pieces()):
            pltpu.make_async_copy(src, dst, w_l.at[i]).start()
            remote(src, dst, w_s.at[i], w_l.at[i], dev(dx, 0, 0, 0)).start()

    for dy in range(1, 4):
        meta_send(dy).wait_recv()
    meta_swap = remote(mt.at[pl.ds(0, 4)], mt.at[pl.ds(4, 4)], mb.at[0], mb.at[1], dev(0, 0, 0, 1))
    meta_swap.start()
    meta_swap.wait_recv()

    i16 = lax.broadcasted_iota(jnp.int32, (PEERS, T), 0)
    xe = (x + lax.shift_right_logical(i16, 2)) & 3
    ze = (z + (i16 & 3)) & 3
    expert = (y * 2 + (xe & 1)) * 16 + ze * 4 + lax.shift_right_logical(xe, 1) * 2 + k
    expert = expert.astype(f32)
    before = (
        lax.broadcasted_iota(jnp.int32, (T, T), 0) < lax.broadcasted_iota(jnp.int32, (T, T), 1)
    ).astype(f32).astype(bf16)
    q = lax.broadcasted_iota(jnp.int32, (ROWS, T), 0)
    q_src = q & 7
    q_slot = lax.shift_right_logical(q, 3).astype(f32)

    def build(s, carry):
        m = mt[s]
        named = jnp.zeros((PEERS, T), f32)
        weight = jnp.zeros((PEERS, T), f32)
        for j in range(4):
            hit = m[j : j + 1, :] == expert
            named = named + jnp.where(hit, 1.0, 0.0)
            weight = weight + jnp.where(hit, m[4 + j : 5 + j, :], 0.0)
        rank = jnp.dot(named.astype(bf16), before, preferred_element_type=f32)
        rank = jnp.where(named > 0.5, rank, -1.0)
        slot = jnp.where(q_src == s, q_slot, -9.0)
        here = rank[:, None, :] == slot[None, :, :]
        cols = pl.ds(pl.multiple_of(s * T, T), T)
        pmat[:, cols] = jnp.where(here, 1.0, 0.0).reshape(ALL, T).astype(bf16)
        scaled = jnp.where(here, weight[:, None, :], 0.0).reshape(ALL, T)
        cmat[cols, :] = scaled.T.astype(bf16)
        return carry

    lax.fori_loop(0, SRC, build, 0)

    acc[...] = jnp.zeros_like(acc)
    sacc[...] = jnp.zeros_like(sacc)

    def out_send(c, i):
        return remote(snd.at[c, i], arr.at[c, i], a_s.at[c], a_r.at[c], dev(i // 4, 0, i % 4, 0))

    def back_send(n, i):
        return remote(
            snd.at[n, i], ret.at[n, i], r_s.at[n], r_r.at[n], dev(4 - i // 4, 0, 4 - i % 4, 0)
        )

    def swap(c):
        return remote(
            tok.at[c, pl.ds(0, 4)], tok.at[c, pl.ds(4, 4)], b_s.at[c], b_r.at[c], dev(0, 0, 0, 1)
        )

    def rows_of(ref, c):
        return ref[c].astype(f32).reshape(ALL, DC).astype(bf16)

    def forward(it, carry):
        @pl.when(it < NC)
        def _():
            c = it
            for dy in range(1, 4):
                gather_send(c, dy).wait_recv()
            swap(c).start()

            @pl.when(c + 2 < NC)
            def _():
                gather_start(c + 2)

            swap(c).wait_recv()
            for h in range(DC // 256):
                cols = slice(h * 256, h * 256 + 256)
                rhs = tok[c, :, :, cols].reshape(SRC * T, 256)
                packed = jnp.dot(pmat[...], rhs, preferred_element_type=f32)
                packed = packed.reshape(PEERS, CAP, SRC, 256).astype(bf16)
                snd[c, :, :, :, cols] = packed
                arr[c, 0, :, :, cols] = packed[0]
            for i in range(1, PEERS):
                out_send(c, i).start()

        @pl.when(it >= LAG_B)
        def _():
            c = it - LAG_B
            slot = c % 2

            @pl.when(c == 0)
            def _():
                for i, (_, dst, _) in enumerate(shared_pieces()):
                    wait_bytes(dst, w_l.at[i])

            sacc[...] += jnp.dot(
                tok[c].reshape(SRC * T, DC), wsh[c], preferred_element_type=f32
            )
            wait_bytes(arr.at[c, pl.ds(1, PEERS - 1)], a_r.at[c])
            stage[...] = rows_of(arr, c)
            for copy in wgu_load(c, slot):
                copy.wait()
            for h in range(2 * FF // 256):
                cols = slice(h * 256, h * 256 + 256)
                acc[:, cols] += jnp.dot(stage[...], wgu[slot, :, cols], preferred_element_type=f32)

            @pl.when(c + 2 < NC)
            def _():
                for copy in wgu_load(c + 2, slot):
                    copy.start()

        return carry

    lax.fori_loop(0, NC + LAG_B, forward, 0)

    def silu_mul(gate, up):
        return (gate / (1.0 + jnp.exp(-gate)) * up).astype(bf16)

    for h in range(FF // 256):
        cols = slice(h * 256, h * 256 + 256)
        hid[:, cols] = silu_mul(acc[:, cols], acc[:, FF + h * 256 : FF + h * 256 + 256])
    shid[...] = silu_mul(sacc[:, 0:128], sacc[:, 128:256])

    def part_send(n):
        return remote(psend.at[n % 2], prcv.at[n], p_s.at[n], p_r.at[n], dev(0, 0, 0, 1))

    def line_send(n, dy):
        return remote(
            ysend.at[n % 2, dy - 1], yrcv.at[n, 3 - dy], y_s.at[n], y_r.at[n], dev(0, dy, 0, 0)
        )

    def backward(it, carry):
        @pl.when(it < NC)
        def _():
            n = it
            slot = n % 2
            wait_bytes(snd.at[n, pl.ds(1, PEERS - 1)], a_s.at[n])
            wdn_load(n, slot).wait()
            for h in range(DC // 256):
                cols = slice(h * 256, h * 256 + 256)
                done = jnp.dot(hid[...], wdn[slot, :, cols], preferred_element_type=f32)
                done = done.reshape(PEERS, CAP, SRC, 256).astype(bf16)
                snd[n, :, :, :, cols] = done
                ret[n, 0, :, :, cols] = done[0]
            for i in range(1, PEERS):
                back_send(n, i).start()

            @pl.when(n + 2 < NC)
            def _():
                wdn_load(n + 2, slot).start()

        @pl.when(jnp.logical_and(it >= LAG_R, it < NC + LAG_R))
        def _():
            n = it - LAG_R

            @pl.when(n >= 2)
            def _():
                part_send(n - 2).wait_send()
                wait_bytes(ysend.at[n % 2], y_s.at[n - 2])

            wait_bytes(ret.at[n, pl.ds(1, PEERS - 1)], r_r.at[n])
            stage[...] = rows_of(ret, n)
            cols = pl.ds(pl.multiple_of(n * DC, DC), DC)
            half = SRC * T // 2
            for lo in (half, 0):
                rows = pl.ds(lo, half)
                part = jnp.dot(cmat[rows, :], stage[...], preferred_element_type=f32)
                part = part + jnp.dot(shid[rows, :], wsd[:, cols], preferred_element_type=f32)
                if lo:
                    psend[n % 2] = part.astype(bf16)
                    part_send(n).start()
                else:
                    kept = part
            part_send(n).wait_recv()
            total = kept + prcv[n].astype(f32)
            for dy in range(1, 4):
                ysend[n % 2, dy - 1] = total[dy * T : dy * T + T].astype(bf16)
                line_send(n, dy).start()
            oacc[n] = total[0:T]

        @pl.when(it >= LAG_R + LAG_F)
        def _():
            n = it - LAG_R - LAG_F
            wait_bytes(yrcv.at[n], y_r.at[n])
            total = oacc[n]
            for j in range(3):
                total = total + yrcv[n, j].astype(f32)
            out_ref[:, pl.ds(pl.multiple_of(n * DC, DC), DC)] = total.astype(bf16)

        return carry

    lax.fori_loop(0, NC + LAG_R + LAG_F, backward, 0)

    for dy in range(1, 4):
        meta_send(dy).wait_send()
    meta_swap.wait_send()

    def drain(c, carry):
        for dy in range(1, 4):
            gather_send(c, dy).wait_send()
        swap(c).wait_send()
        wait_bytes(snd.at[c, pl.ds(1, PEERS - 1)], r_s.at[c])
        return carry

    lax.fori_loop(0, NC, drain, 0)
    for n in (NC - 2, NC - 1):
        part_send(n).wait_send()
        wait_bytes(ysend.at[n % 2], y_s.at[n])

    @pl.when(native)
    def _():
        for i, (src, dst, dx) in enumerate(shared_pieces()):
            remote(src, dst, w_s.at[i], w_l.at[i], dev(dx, 0, 0, 0)).wait_send()


def per_device(tokens, ids, weights, gate, up, down, sgate, sup, sdown):
    meta = jnp.concatenate([ids.T.astype(f32), weights.T], axis=0)
    dma = pltpu.SemaphoreType.DMA
    half = SRC * T // 2
    scratch = [
        pltpu.VMEM((NC, SRC, T, DC), bf16),
        pltpu.VMEM((NC, PEERS, CAP, SRC, DC), bf16),
        pltpu.VMEM((NC, PEERS, CAP, SRC, DC), bf16),
        pltpu.VMEM((NC, PEERS, CAP, SRC, DC), bf16),
        pltpu.VMEM((ALL, DC), bf16),
        pltpu.VMEM((ALL, 2 * FF), f32),
        pltpu.VMEM((ALL, FF), bf16),
        pltpu.VMEM((ALL, SRC * T), bf16),
        pltpu.VMEM((SRC * T, ALL), bf16),
        pltpu.VMEM((2, DC, 2 * FF), bf16),
        pltpu.VMEM((2, FF, DC), bf16),
        pltpu.VMEM((NC, DC, 256), bf16),
        pltpu.VMEM((128, D), bf16),
        pltpu.VMEM((SRC * T, 256), f32),
        pltpu.VMEM((SRC * T, 128), bf16),
        pltpu.VMEM((2, half, DC), bf16),
        pltpu.VMEM((NC, half, DC), bf16),
        pltpu.VMEM((2, 3, T, DC), bf16),
        pltpu.VMEM((NC, 3, T, DC), bf16),
        pltpu.VMEM((NC, T, DC), f32),
        pltpu.VMEM((SRC, 8, T), f32),
        dma((NC,)),
        dma((NC, 4)),
        dma((NC, 4)),
        dma((NC,)),
        dma((NC,)),
        dma,
        dma((4,)),
        dma((4,)),
        dma((2,)),
        dma((NC,)),
        dma((NC,)),
        dma((NC,)),
        dma((NC,)),
        dma((4,)),
        dma((4,)),
        dma((2, 2)),
        dma((2,)),
        dma((NC,)),
        dma((NC,)),
        dma((NC,)),
        dma((NC,)),
    ]
    hbm = pl.BlockSpec(memory_space=pl.ANY)
    return pl.pallas_call(
        kernel,
        out_shape=jax.ShapeDtypeStruct((T, D), bf16),
        in_specs=[hbm] * 8,
        out_specs=pl.BlockSpec(memory_space=pltpu.VMEM),
        scratch_shapes=scratch,
        cost_estimate=pl.CostEstimate(
            flops=2 * ALL * D * 3 * FF + 2 * SRC * T * D * 3 * 128,
            bytes_accessed=3 * D * FF * 2 + 4 * T * D,
            transcendentals=ALL * FF,
        ),
        compiler_params=pltpu.CompilerParams(
            collective_id=1, has_side_effects=True, vmem_limit_bytes=60 * 2**20
        ),
    )(
        tokens, meta, gate[0], up[0], down[0],
        sgate.reshape(NC, DC, 128), sup.reshape(NC, DC, 128), sdown,
    )


def solution(mesh):
    both = ("row", "col")
    placed = (
        P(both, None),
        P(both, None),
        P(both, None),
        P(both, None, None),
        P(both, None, None),
        P(both, None, None),
        P(None, "row"),
        P(None, "row"),
        P("row", None),
    )
    return jax.shard_map(
        per_device, mesh=mesh, in_specs=placed, out_specs=P(both, None), check_vma=False
    )
```

time: 590 us -> 153 us (0.26); the launches traced: 584 us -> 152 us
  waiting for transfers between devices: 320 us -> 0 us
  Pallas kernels: 0 us -> 148 us
  blocking collectives: 112 us -> 0 us
  local copies, waits for them, and re-layouts: 59.9 us -> 2.16 us
  matrix products: 50.9 us -> 0 us
  other arithmetic: 15.4 us -> 1.96 us
  between operations: 13.3 us -> 0.01 us
  starting transfers between devices: 11.9 us -> 0 us
    all_gather x1 -> x0, waiting for transfers between devices: 154 us -> none  [per_device(): shard_rows = lax.all_gather(tokens, ROW, axis=0, tiled=True)]
    pallas_call x0 -> x1, Pallas kernels: none -> 148 us  [per_device(): pl.pallas_call(kernel, out_shape=jax.ShapeDtypeStruct((T, D), bf16), in_s...]
    all_to_all x1 -> x0, blocking collectives: 112 us -> none  [per_device(): lax.all_to_all(outgoing.reshape(experts, capacity, model_width), ROW_COL,...]
    all_to_all x1 -> x0, waiting for transfers between devices: 96.6 us -> none  [per_device(): lax.all_to_all(results.reshape(experts, capacity, model_width), ROW_COL,...]
    reduce_scatter x2 -> x0, waiting for transfers between devices: 69.2 us -> none  [own_rows(): running = lax.psum_scatter(running, axis, scatter_dimension=0, tiled=True)]
    dot_general x4 -> x0, matrix products: 50.9 us -> none  [the longest x1 18.8 us: expert_mlp(): jnp.dot(hidden, down_w, preferred_element_type=jnp.float32)]
    reshape x3 -> x0, local copies, waits for them, and re-layouts: 24.2 us -> none  [the longest x1 8.26 us: per_device(): arrived.reshape(-1, model_width)]
    gather x3 -> x0, local copies, waits for them, and re-layouts: 24.1 us -> none  [the longest x2 13.3 us: per_device(): tokens[jnp.maximum(source_table, 0)]]
  transfers between devices with their start and end apart: 4 -> 0, of which waited for: 3 -> 0; matrix products, arithmetic and copies ran while one was open for 17% -> 0% of each run, Pallas kernels for 0% -> 0%
where the time goes in v1:
time: 153 us; the launch traced here: 152 us
  Pallas kernels  148 us (97%)
  local copies, waits for them, and re-layouts  2.16 us (1%)
  other arithmetic  1.96 us (1%)
    pallas_call x1, Pallas kernels, per_device(): pl.pallas_call(kernel, out_shape=jax.ShapeDtypeStruct((T, D), bf16), in_s...  148 us

profile of v1, /device:TPU:1, one launch (start us, length us, event | category | flops | bytes accessed | tf_op | source)
XLA Modules:
  0.0 152.4 jit_solution(13884313651383130244)
XLA Ops:
  0.0 0.7 convert_bitcast_fusion
  0.7 1.3 pad_maximum_fusion.meta_hbm
  2.0 148.3 %shard_map.91 = bf16[128,3584]{1,0:T(8,128)(2,1)} custom-call(bf16[128,3584]{1,0:T(8,128)(2,1)} %tok_hbm.1, f32[8,128]{1,0:T(8,128)} %pad_maximum_fusion.meta_hbm, bf16[3584,1024]{1,0:T(8,128)(2,1)} %bitcast.9, bf16[3584,1024]{1,0:T(8,128)(2,1)} %bitcast.10, bf16[1024,3584]{1,0:T(8,128)(2,1)} %bitcast.11, bf16[7,512,128]{2,1,0:T(8,128)(2,1)} %bitcast.12, ...), custom_call_target="tpu_custom_call" | custom-call | flops 16911433728 | bytes 23855104 | tf_op jit(solution)/shard_map/pallas_call | solution.py:384
  150.3 2.2 %copy.11 = bf16[128,3584]{1,0:T(8,128)(2,1)} copy(bf16[128,3584]{1,0:T(8,128)(2,1)} %shard_map.91) | data formatting | bytes 1835008

commit v2 on v1

v2 whole, which is shorter than its diff:
```python
import functools

import jax
import jax.numpy as jnp
from jax import lax
from jax.experimental import pallas as pl
from jax.experimental.pallas import tpu as pltpu
from jax.sharding import PartitionSpec as P

D = 3584
FF = 1024
T = 128
CAP = 5
DC = 256
NC = D // DC
PEERS = 16
SRC = 8
CUT = 3
RA = PEERS * CUT * SRC
ALL = PEERS * CAP * SRC
WHOLE_F = 8
SPLIT_R = 4
SLOTS_GU = NC - WHOLE_F
SLOTS_D = SPLIT_R
LAG_B = 3
LAG_R = 4
LAG_F = 3
LAG_S = 4
KEEP = 4
MESH = pl.DeviceIdType.MESH
bf16 = jnp.bfloat16
f32 = jnp.float32


def kernel(
    tok_hbm, ids_hbm, cw_hbm, wg_hbm, wu_hbm, wd_hbm, sg_hbm, su_hbm, sd_hbm,
    out_ref,
    tok, snd, arr, ret, stage, acc, hid, pmat, cmat, wgu, wdn, wsh, wsd, sacc, shid,
    psend, prcv, ysend, yrcv, oacc, mt, ids_v, cw_v,
    ld, g_s, g_r, b_s, b_r, m_l, m_s, m_r, a_s, a_r, a_b, r_s, r_r, r_b, w_s, w_l, wg_l, wd_l, p_s, p_r, y_s, y_r,
):
    row = lax.axis_index("row")
    col = lax.axis_index("col")
    y, x_lo = row // 2, row % 2
    z, x_hi, k = col // 4, (col // 2) % 2, col % 2
    x = x_hi * 2 + x_lo

    def dev(dx, dy, dz, dk):
        xx, yy, zz, kk = (x + dx) % 4, (y + dy) % 4, (z + dz) % 4, (k + dk) % 2
        return (yy * 2 + xx % 2, zz * 4 + (xx // 2) * 2 + kk)

    def remote(src, dst, ssem, rsem, where):
        return pltpu.make_async_remote_copy(
            src, dst, ssem, rsem, device_id=where, device_id_type=MESH
        )

    def wait_bytes(ref, sem):
        pltpu.make_async_copy(ref, ref, sem).wait()

    native = x_lo == k

    barrier = pltpu.get_barrier_semaphore()
    plane = [(i // 4, 0, i % 4, 0) for i in range(1, PEERS)]
    line = [(0, dy, 0, dk) for dk in range(2) for dy in range(4)][1:]
    for offset in plane + line:
        pl.semaphore_signal(barrier, inc=1, device_id=dev(*offset), device_id_type=MESH)

    def tok_load(c):
        return pltpu.make_async_copy(
            tok_hbm.at[:, pl.ds(c * DC, DC)], tok.at[c, 0], ld.at[c]
        )

    meta_copies = (
        pltpu.make_async_copy(ids_hbm, ids_v, m_l.at[0]),
        pltpu.make_async_copy(cw_hbm, cw_v, m_l.at[1]),
    )
    for copy in meta_copies:
        copy.start()
    for c in range(NC):
        tok_load(c).start()

    def wgu_load(c, slot):
        rows = pl.ds(c * DC, DC)
        return (
            pltpu.make_async_copy(wg_hbm.at[rows, :], wgu.at[slot, :, pl.ds(0, FF)], wg_l.at[slot, 0]),
            pltpu.make_async_copy(wu_hbm.at[rows, :], wgu.at[slot, :, pl.ds(FF, FF)], wg_l.at[slot, 1]),
        )

    def wdn_load(n, slot):
        return pltpu.make_async_copy(
            wd_hbm.at[:, pl.ds(n * DC, DC)], wdn.at[slot], wd_l.at[slot]
        )

    acc[...] = jnp.zeros_like(acc)
    sacc[...] = jnp.zeros_like(sacc)
    for copy in meta_copies:
        copy.wait()
    mt[0, 0:4, :] = ids_v[...].astype(f32)
    mt[0, 4:8, :] = cw_v[...]
    pl.semaphore_wait(barrier, len(plane + line))

    def meta_send(j):
        dk, dy = j // 4, j % 4
        there = dk * 4 + (4 - dy) % 4
        return remote(mt.at[0], mt.at[there], m_s.at[j], m_r.at[there], dev(0, dy, 0, dk))

    for j in range(1, SRC):
        meta_send(j).start()

    def gather_send(c, dy):
        return remote(
            tok.at[c, 0], tok.at[c, 4 - dy], g_s.at[c, dy], g_r.at[c, 4 - dy], dev(0, dy, 0, 0)
        )

    def gather_start(c):
        tok_load(c).wait()
        for dy in range(1, 4):
            gather_send(c, dy).start()

    gather_start(0)

    GATE, UP, DOWN = range(3)

    def quarter(w, q):
        if w == GATE:
            return sg_hbm.at[:, q], wsh.at[0, :, q]
        if w == UP:
            return su_hbm.at[:, q], wsh.at[1, :, q]
        return sd_hbm.at[q], wsd.at[q]

    def across_x(w):
        moves = ((0, 1), (1, 1), (2, 3), (3, 3))
        return [
            remote(*quarter(w, q), w_s.at[q, w], w_l.at[q, w], dev(dx, 0, 0, 0)) for q, dx in moves
        ]

    def own(w):
        return [pltpu.make_async_copy(*quarter(w, q), w_l.at[q, w]) for q in range(4)]

    def weight_wait(w, qs):
        for q in qs:
            wait_bytes(quarter(w, q)[1], w_l.at[q, w])

    def rest_wait(w):
        weight_wait(w, range(4))

    @pl.when(native)
    def _():
        for w in (UP, GATE):
            for copy in across_x(w):
                copy.start()

    gather_start(1)
    for slot in range(SLOTS_GU):
        for copy in wgu_load(slot, slot):
            copy.start()
    for slot in range(SLOTS_D):
        wdn_load(slot, slot).start()

    @pl.when(native)
    def _():
        for w in (UP, GATE, DOWN):
            for copy in own(w):
                copy.start()

    gather_start(2)
    for j in range(1, SRC):
        meta_send(j).wait_recv()

    i16 = lax.broadcasted_iota(jnp.int32, (PEERS, T), 0)
    xe = (x + lax.shift_right_logical(i16, 2)) & 3
    ze = (z + (i16 & 3)) & 3
    expert = (y * 2 + (xe & 1)) * 16 + ze * 4 + lax.shift_right_logical(xe, 1) * 2 + k
    expert = expert.astype(f32)
    before = (
        lax.broadcasted_iota(jnp.int32, (T, T), 0) < lax.broadcasted_iota(jnp.int32, (T, T), 1)
    ).astype(f32).astype(bf16)
    parts = ((0, CUT, 0, RA), (CUT, CAP, RA, ALL))

    def build(s, carry):
        m = mt[s]
        named = jnp.zeros((PEERS, T), f32)
        weight = jnp.zeros((PEERS, T), f32)
        for j in range(4):
            hit = m[j : j + 1, :] == expert
            named = named + jnp.where(hit, 1.0, 0.0)
            weight = weight + jnp.where(hit, m[4 + j : 5 + j, :], 0.0)
        rank = jnp.dot(named.astype(bf16), before, preferred_element_type=f32)
        rank = jnp.where(named > 0.5, rank, -1.0)
        cols = pl.ds(pl.multiple_of(s * T, T), T)
        for s0, s1, r0, r1 in parts:
            q = lax.broadcasted_iota(jnp.int32, ((s1 - s0) * SRC, T), 0)
            q_slot = lax.shift_right_logical(q, 3).astype(f32) + s0
            slot = jnp.where((q & 7) == s, q_slot, -9.0)
            here = rank[:, None, :] == slot[None, :, :]
            pmat[r0:r1, cols] = jnp.where(here, 1.0, 0.0).reshape(r1 - r0, T).astype(bf16)
            scaled = jnp.where(here, weight[:, None, :], 0.0).reshape(r1 - r0, T)
            cmat[cols, r0:r1] = scaled.T.astype(bf16)
        return carry

    lax.fori_loop(0, SRC, build, 0)

    def out_send(c, i, s0, s1, sem):
        slots = pl.ds(s0, s1 - s0)
        return remote(snd.at[c, i, slots], arr.at[c, i, slots], a_s.at[c], sem.at[c], dev(i // 4, 0, i % 4, 0))

    def back_send(n, i, s0, s1, sem):
        slots = pl.ds(s0, s1 - s0)
        return remote(snd.at[n, i, slots], ret.at[n, i, slots], r_s.at[n], sem.at[n], dev(4 - i // 4, 0, 4 - i % 4, 0))

    def swap(c):
        return remote(
            tok.at[c, pl.ds(0, 4)], tok.at[c, pl.ds(4, 4)], b_s.at[c], b_r.at[c], dev(0, 0, 0, 1)
        )

    def put(ref, c, values, which):
        for s0, s1, r0, r1 in which:
            base = which[0][2]
            ref[c, :, s0:s1] = values[r0 - base : r1 - base].reshape(PEERS, s1 - s0, SRC, DC).astype(bf16)

    def put_own(ref, c, values, which):
        for s0, s1, r0, r1 in which:
            base = r0 - which[0][2]
            ref[c, 0, s0:s1] = values[base : base + (s1 - s0) * SRC].reshape(s1 - s0, SRC, DC).astype(bf16)

    def take(ref, c, which):
        for s0, s1, r0, r1 in which:
            stage[r0:r1, :] = ref[c, :, s0:s1].astype(f32).reshape(r1 - r0, DC).astype(bf16)

    def line_wait(c):
        for dy in range(1, 4):
            gather_send(c, dy).wait_recv()
        swap(c).start()

    line_wait(0)
    gather_start(3)

    peers = pl.ds(1, PEERS - 1)

    def expert_dot(slot, r0, r1):
        for h in range(2 * FF // 256):
            cols = slice(h * 256, h * 256 + 256)
            acc[r0:r1, cols] += jnp.dot(stage[r0:r1, :], wgu[slot, :, cols], preferred_element_type=f32)

    def shared_dot(c):
        weights = jnp.concatenate([wsh[j, c].reshape(DC, 128) for j in range(2)], axis=1)
        sacc[...] += jnp.dot(tok[c].reshape(SRC * T, DC), weights, preferred_element_type=f32)

    def forward(it, carry):
        @pl.when(it < NC)
        def _():
            c = it
            swap(c).wait_recv()
            packed = jnp.dot(pmat[...], tok[c].reshape(SRC * T, DC), preferred_element_type=f32)
            put(snd, c, packed, parts)
            put_own(arr, c, packed, parts)

            @pl.when(c < WHOLE_F)
            def _():
                for i in range(1, PEERS):
                    out_send(c, i, 0, CAP, a_r).start()

            @pl.when(c >= WHOLE_F)
            def _():
                for i in range(1, PEERS):
                    out_send(c, i, 0, CUT, a_r).start()

            @pl.when(c == NC - 1)
            def _():
                def rest(cc, carry):
                    for i in range(1, PEERS):
                        out_send(cc, i, CUT, CAP, a_b).start()
                    return carry

                lax.fori_loop(WHOLE_F, NC, rest, 0)

            @pl.when(jnp.logical_and(c == 3, native))
            def _():
                for copy in across_x(DOWN):
                    copy.start()

            @pl.when(c + 1 < NC)
            def _():
                line_wait(c + 1)

            @pl.when(c + 4 < NC)
            def _():
                gather_start(c + 4)

        @pl.when(it >= LAG_B)
        def _():
            c = it - LAG_B
            slot = c % SLOTS_GU

            @pl.when(c == LAG_S)
            def _():
                rest_wait(UP)
                rest_wait(GATE)

            @pl.when(c >= LAG_S)
            def _():
                shared_dot(c - LAG_S)

            for copy in wgu_load(c, slot):
                copy.wait()

            @pl.when(c < WHOLE_F)
            def _():
                wait_bytes(arr.at[c, peers], a_r.at[c])
                take(arr, c, parts)
                expert_dot(slot, 0, ALL)

                @pl.when(c + SLOTS_GU < NC)
                def _():
                    for copy in wgu_load(c + SLOTS_GU, slot):
                        copy.start()

            @pl.when(c >= WHOLE_F)
            def _():
                wait_bytes(arr.at[c, peers, pl.ds(0, CUT)], a_r.at[c])
                take(arr, c, parts[:1])
                expert_dot(slot, 0, RA)

        return carry

    lax.fori_loop(0, NC + LAG_B, forward, 0)

    def silu_mul(gate, up):
        return (gate / (1.0 + jnp.exp(-gate)) * up).astype(bf16)

    def activate(r0, r1):
        for h in range(FF // 256):
            cols = slice(h * 256, h * 256 + 256)
            hid[r0:r1, cols] = silu_mul(acc[r0:r1, cols], acc[r0:r1, FF + h * 256 : FF + h * 256 + 256])

    def down(n, which, sem):
        slot = n % SLOTS_D
        done = jnp.dot(hid[which[0][2] : which[-1][3], :], wdn[slot], preferred_element_type=f32)
        put(snd, n, done, which)
        put_own(ret, n, done, which)
        for i in range(1, PEERS):
            back_send(n, i, which[0][0], which[-1][1], sem).start()

    activate(0, RA)

    def down_a(n, carry):
        wait_bytes(snd.at[n, peers], a_s.at[n])
        wdn_load(n, n).wait()
        down(n, parts[:1], r_r)
        return carry

    lax.fori_loop(0, SPLIT_R, down_a, 0)
    def shared_rest(c, carry):
        shared_dot(c)
        return carry

    lax.fori_loop(NC - LAG_S, NC, shared_rest, 0)
    shid[...] = silu_mul(sacc[:, 0:128], sacc[:, 128:256])

    def late(c, carry):
        wait_bytes(arr.at[c, peers, pl.ds(CUT, CAP - CUT)], a_b.at[c])
        take(arr, c, parts[1:])
        expert_dot(c % SLOTS_GU, RA, ALL)
        return carry

    lax.fori_loop(WHOLE_F, NC, late, 0)
    activate(RA, ALL)

    def down_b(n, carry):
        down(n, parts[1:], r_b)
        wdn_load(n + SLOTS_D, n).start()
        return carry

    lax.fori_loop(0, SPLIT_R, down_b, 0)

    def part_send(n):
        return remote(psend.at[n % 2], prcv.at[n], p_s.at[n], p_r.at[n], dev(0, 0, 0, 1))

    def line_send(n, dy):
        return remote(
            ysend.at[n % KEEP, dy - 1], yrcv.at[n, 3 - dy], y_s.at[n], y_r.at[n], dev(0, dy, 0, 0)
        )

    half = SRC * T // 2

    def backward(it, carry):
        @pl.when(it < NC)
        def _():
            n = it
            slot = n % SLOTS_D
            wait_bytes(snd.at[n, peers], a_s.at[n])
            wdn_load(n, slot).wait()
            down(n, parts, r_r)

            @pl.when(n + SLOTS_D < NC)
            def _():
                wdn_load(n + SLOTS_D, slot).start()

        @pl.when(jnp.logical_and(it >= LAG_R + 1, it < NC + LAG_R + 1))
        def _():
            n = it - LAG_R - 1

            @pl.when(n >= KEEP)
            def _():
                wait_bytes(ysend.at[n % KEEP], y_s.at[n - KEEP])

            part_send(n).wait_recv()
            for dy in range(1, 4):
                rows = slice(dy * T, dy * T + T)
                ysend[n % KEEP, dy - 1] = (oacc[n % KEEP, rows] + prcv[n, rows].astype(f32)).astype(bf16)
                line_send(n, dy).start()

        @pl.when(it >= LAG_R + 1 + LAG_F)
        def _():
            n = it - LAG_R - 1 - LAG_F
            wait_bytes(yrcv.at[n], y_r.at[n])
            total = oacc[n % KEEP, 0:T] + prcv[n, 0:T].astype(f32)
            for j in range(3):
                total = total + yrcv[n, j].astype(f32)
            out_ref[:, pl.ds(pl.multiple_of(n * DC, DC), DC)] = total.astype(bf16)

        @pl.when(jnp.logical_and(it >= LAG_R, it < NC + LAG_R))
        def _():
            n = it - LAG_R

            @pl.when(n >= 2)
            def _():
                part_send(n - 2).wait_send()

            @pl.when(n < SPLIT_R)
            def _():
                wait_bytes(ret.at[n, peers, pl.ds(0, CUT)], r_r.at[n])
                wait_bytes(ret.at[n, peers, pl.ds(CUT, CAP - CUT)], r_b.at[n])

            @pl.when(n >= SPLIT_R)
            def _():
                wait_bytes(ret.at[n, peers], r_r.at[n])

            take(ret, n, parts)

            @pl.when(n == 0)
            def _():
                rest_wait(DOWN)

            cols = pl.ds(pl.multiple_of(n * DC, DC), DC)
            for lo in (half, 0):
                rows = pl.ds(lo, half)
                part = jnp.dot(cmat[rows, :], stage[...], preferred_element_type=f32)
                part = part + jnp.dot(
                    shid[rows, :], wsd[:, :, cols].reshape(128, DC), preferred_element_type=f32
                )
                if lo:
                    psend[n % 2] = part.astype(bf16)
                    part_send(n).start()
                else:
                    oacc[n % KEEP] = part

        return carry

    lax.fori_loop(SPLIT_R, NC + LAG_R + 1 + LAG_F, backward, 0)

    for j in range(1, SRC):
        meta_send(j).wait_send()

    def drain(c, carry):
        for dy in range(1, 4):
            gather_send(c, dy).wait_send()
        swap(c).wait_send()
        wait_bytes(snd.at[c, peers], r_s.at[c])
        return carry

    lax.fori_loop(0, NC, drain, 0)
    for n in (NC - 2, NC - 1):
        part_send(n).wait_send()
    for n in range(NC - KEEP, NC):
        wait_bytes(ysend.at[n % KEEP], y_s.at[n])

    @pl.when(native)
    def _():
        for w in (UP, GATE, DOWN):
            for copy in across_x(w):
                copy.wait_send()


def per_device(tokens, ids, weights, gate, up, down, sgate, sup, sdown):
    dma = pltpu.SemaphoreType.DMA
    half = SRC * T // 2
    scratch = [
        pltpu.VMEM((NC, SRC, T, DC), bf16),
        pltpu.VMEM((NC, PEERS, CAP, SRC, DC), bf16),
        pltpu.VMEM((NC, PEERS, CAP, SRC, DC), bf16),
        pltpu.VMEM((NC, PEERS, CAP, SRC, DC), bf16),
        pltpu.VMEM((ALL, DC), bf16),
        pltpu.VMEM((ALL, 2 * FF), f32),
        pltpu.VMEM((ALL, FF), bf16),
        pltpu.VMEM((ALL, SRC * T), bf16),
        pltpu.VMEM((SRC * T, ALL), bf16),
        pltpu.VMEM((SLOTS_GU, DC, 2 * FF), bf16),
        pltpu.VMEM((SLOTS_D, FF, DC), bf16),
        pltpu.VMEM((2, NC, 4, DC // 4, 128), bf16),
        pltpu.VMEM((4, 32, D), bf16),
        pltpu.VMEM((SRC * T, 256), f32),
        pltpu.VMEM((SRC * T, 128), bf16),
        pltpu.VMEM((2, half, DC), bf16),
        pltpu.VMEM((NC, half, DC), bf16),
        pltpu.VMEM((KEEP, 3, T, DC), bf16),
        pltpu.VMEM((NC, 3, T, DC), bf16),
        pltpu.VMEM((KEEP, half, DC), f32),
        pltpu.VMEM((SRC, 8, T), f32),
        pltpu.VMEM((4, T), jnp.int32),
        pltpu.VMEM((4, T), f32),
        dma((NC,)),
        dma((NC, 4)),
        dma((NC, 4)),
        dma((NC,)),
        dma((NC,)),
        dma((2,)),
        dma((SRC,)),
        dma((SRC,)),
        dma((NC,)),
        dma((NC,)),
        dma((NC,)),
        dma((NC,)),
        dma((NC,)),
        dma((NC,)),
        dma((4, 3)),
        dma((4, 3)),
        dma((SLOTS_GU, 2)),
        dma((SLOTS_D,)),
        dma((NC,)),
        dma((NC,)),
        dma((NC,)),
        dma((NC,)),
    ]
    hbm = pl.BlockSpec(memory_space=pl.ANY)
    return pl.pallas_call(
        kernel,
        out_shape=jax.ShapeDtypeStruct((T, D), bf16),
        in_specs=[hbm] * 9,
        out_specs=pl.BlockSpec(memory_space=pltpu.VMEM),
        scratch_shapes=scratch,
        cost_estimate=pl.CostEstimate(
            flops=2 * ALL * D * 3 * FF + 2 * SRC * T * D * 3 * 128,
            bytes_accessed=3 * D * FF * 2 + 4 * T * D,
            transcendentals=ALL * FF,
        ),
        compiler_params=pltpu.CompilerParams(
            collective_id=1, has_side_effects=True, vmem_limit_bytes=60 * 2**20
        ),
    )(
        tokens, ids.T, weights.T, gate[0], up[0], down[0],
        sgate.reshape(NC, 4, DC // 4, 128), sup.reshape(NC, 4, DC // 4, 128), sdown.reshape(4, 32, D),
    )


def solution(mesh):
    both = ("row", "col")
    placed = (
        P(both, None),
        P(both, None),
        P(both, None),
        P(both, None, None),
        P(both, None, None),
        P(both, None, None),
        P(None, "row"),
        P(None, "row"),
        P("row", None),
    )
    return jax.shard_map(
        per_device, mesh=mesh, in_specs=placed, out_specs=P(both, None), check_vma=False
    )
```

time: 153 us -> 144 us (0.941)
  Pallas kernels: 148 us -> 141 us
  other arithmetic: 1.96 us -> 0 us
    pallas_call x1, Pallas kernels: 148 us -> 141 us  [per_device(): pl.pallas_call(kernel, out_shape=jax.ShapeDtypeStruct((T, D), bf16), in_s...]
where the time goes in v2:
time: 144 us; the launch traced here: 143 us
  Pallas kernels  141 us (98%)
  local copies, waits for them, and re-layouts  2.16 us (2%)
    pallas_call x1, Pallas kernels, per_device(): pl.pallas_call(kernel, out_shape=jax.ShapeDtypeStruct((T, D), bf16), in_s...  141 us

profile of v2, /device:TPU:1, one launch (start us, length us, event | category | flops | bytes accessed | tf_op | source)
XLA Modules:
  0.0 143.4 jit_solution(14061671818695805324)
XLA Ops:
  0.0 141.3 %shard_map.91 = bf16[128,3584]{1,0:T(8,128)(2,1)} custom-call(bf16[128,3584]{1,0:T(8,128)(2,1)} %tok_hbm.1, s32[4,128]{1,0:T(4,128)} %bitcast.14, f32[4,128]{1,0:T(4,128)} %bitcast.15, bf16[3584,1024]{1,0:T(8,128)(2,1)} %bitcast.8, bf16[3584,1024]{1,0:T(8,128)(2,1)} %bitcast.9, bf16[1024,3584]{1,0:T(8,128)(2,1)} %bitcast.10, ...), custom_call_target="tpu_custom_call" | custom-call | flops 16911433728 | bytes 23855104 | tf_op jit(solution)/shard_map/pallas_call | solution.py:536
  141.3 2.2 %copy.11 = bf16[128,3584]{1,0:T(8,128)(2,1)} copy(bf16[128,3584]{1,0:T(8,128)(2,1)} %shard_map.91) | data formatting | bytes 1835008

commit v3 on v2

--- a/solution.py
+++ b/solution.py
@@ -18,10 +18,10 @@
 CUT = 3
 RA = PEERS * CUT * SRC
 ALL = PEERS * CAP * SRC
-WHOLE_F = 8
-SPLIT_R = 4
-SLOTS_GU = NC - WHOLE_F
-SLOTS_D = SPLIT_R
+WHOLE_F = 13
+SPLIT_R = 1
+SLOTS_GU = 6
+SLOTS_D = 4
 LAG_B = 3
 LAG_R = 4
 LAG_F = 3
@@ -274,10 +274,10 @@
 
                 lax.fori_loop(WHOLE_F, NC, rest, 0)
 
-            @pl.when(jnp.logical_and(c == 3, native))
-            def _():
-                for copy in across_x(DOWN):
-                    copy.start()
+                @pl.when(native)
+                def _():
+                    for copy in across_x(DOWN):
+                        copy.start()
 
             @pl.when(c + 1 < NC)
             def _():

time: 144 us -> 142 us (0.986)
  Pallas kernels: 141 us -> 139 us
    pallas_call x1, Pallas kernels: 141 us -> 139 us  [per_device(): pl.pallas_call(kernel, out_shape=jax.ShapeDtypeStruct((T, D), bf16), in_s...]
where the time goes in v3:
time: 142 us
  Pallas kernels  139 us (98%)
  local copies, waits for them, and re-layouts  2.16 us (2%)
    pallas_call x1, Pallas kernels, per_device(): pl.pallas_call(kernel, out_shape=jax.ShapeDtypeStruct((T, D), bf16), in_s...  139 us

profile of v3, /device:TPU:1, one launch (start us, length us, event | category | flops | bytes accessed | tf_op | source)
XLA Modules:
  0.0 141.5 jit_solution(13397875377644859972)
XLA Ops:
  0.0 139.3 %shard_map.91 = bf16[128,3584]{1,0:T(8,128)(2,1)} custom-call(bf16[128,3584]{1,0:T(8,128)(2,1)} %tok_hbm.1, s32[4,128]{1,0:T(4,128)} %bitcast.14, f32[4,128]{1,0:T(4,128)} %bitcast.15, bf16[3584,1024]{1,0:T(8,128)(2,1)} %bitcast.8, bf16[3584,1024]{1,0:T(8,128)(2,1)} %bitcast.9, bf16[1024,3584]{1,0:T(8,128)(2,1)} %bitcast.10, ...), custom_call_target="tpu_custom_call" | custom-call | flops 16911433728 | bytes 23855104 | tf_op jit(solution)/shard_map/pallas_call | solution.py:536
  139.4 2.2 %copy.11 = bf16[128,3584]{1,0:T(8,128)(2,1)} copy(bf16[128,3584]{1,0:T(8,128)(2,1)} %shard_map.91) | data formatting | bytes 1835008

commit v4 on v3

--- a/solution.py
+++ b/solution.py
@@ -27,6 +27,7 @@
 LAG_F = 3
 LAG_S = 4
 KEEP = 4
+ORDER = sorted(range(1, PEERS), key=lambda i: -(min(i // 4, 4 - i // 4) + min(i % 4, 4 - i % 4)))
 MESH = pl.DeviceIdType.MESH
 bf16 = jnp.bfloat16
 f32 = jnp.float32
@@ -257,18 +258,18 @@
 
             @pl.when(c < WHOLE_F)
             def _():
-                for i in range(1, PEERS):
+                for i in ORDER:
                     out_send(c, i, 0, CAP, a_r).start()
 
             @pl.when(c >= WHOLE_F)
             def _():
-                for i in range(1, PEERS):
+                for i in ORDER:
                     out_send(c, i, 0, CUT, a_r).start()
 
             @pl.when(c == NC - 1)
             def _():
                 def rest(cc, carry):
-                    for i in range(1, PEERS):
+                    for i in ORDER:
                         out_send(cc, i, CUT, CAP, a_b).start()
                     return carry
 
@@ -338,7 +339,7 @@
         done = jnp.dot(hid[which[0][2] : which[-1][3], :], wdn[slot], preferred_element_type=f32)
         put(snd, n, done, which)
         put_own(ret, n, done, which)
-        for i in range(1, PEERS):
+        for i in ORDER:
             back_send(n, i, which[0][0], which[-1][1], sem).start()
 
     activate(0, RA)

time: 142 us -> 141 us (level)
    pallas_call x1, Pallas kernels: 139 us -> 138 us  [per_device(): pl.pallas_call(kernel, out_shape=jax.ShapeDtypeStruct((T, D), bf16), in_s...]
where the time goes in v4:
time: 141 us; the launch traced here: 140 us
  Pallas kernels  138 us (98%)
  local copies, waits for them, and re-layouts  2.16 us (2%)
    pallas_call x1, Pallas kernels, per_device(): pl.pallas_call(kernel, out_shape=jax.ShapeDtypeStruct((T, D), bf16), in_s...  138 us

profile of v4, /device:TPU:1, one launch (start us, length us, event | category | flops | bytes accessed | tf_op | source)
XLA Modules:
  0.0 139.9 jit_solution(14309319047065227785)
XLA Ops:
  0.0 137.8 %shard_map.91 = bf16[128,3584]{1,0:T(8,128)(2,1)} custom-call(bf16[128,3584]{1,0:T(8,128)(2,1)} %tok_hbm.1, s32[4,128]{1,0:T(4,128)} %bitcast.14, f32[4,128]{1,0:T(4,128)} %bitcast.15, bf16[3584,1024]{1,0:T(8,128)(2,1)} %bitcast.8, bf16[3584,1024]{1,0:T(8,128)(2,1)} %bitcast.9, bf16[1024,3584]{1,0:T(8,128)(2,1)} %bitcast.10, ...), custom_call_target="tpu_custom_call" | custom-call | flops 16911433728 | bytes 23855104 | tf_op jit(solution)/shard_map/pallas_call | solution.py:537
  137.8 2.2 %copy.11 = bf16[128,3584]{1,0:T(8,128)(2,1)} copy(bf16[128,3584]{1,0:T(8,128)(2,1)} %shard_map.91) | data formatting | bytes 1835008
